TPU v7x, 512 devices: a whole 4x4x16 slice. The times are simulated.
512 devices in a mesh: blk: 8 (over x, core), pair: 2 (over y_lo), dp: 32 (over y_hi, z).
Axes of the slice: x: 4, y: 4 (y_hi: 2, y_lo: 2; y = y_hi * 2 + y_lo), z: 16, core: 2. Of those that a mesh axis runs over, the one named last changes fastest.
Arguments:
- acts: bfloat16 [4096, 8192], P('dp'), may hold values from -6 to 6
- grads: bfloat16 [4096, 8192], P('dp'), may hold values from -1.5 to 1.5
- basis_in: float32 [8192, 4096], P('dp', ('blk', 'pair')), may hold values from -0.0625 to 0.0625
- basis_out: float32 [8192, 4096], P('dp', ('blk', 'pair')), may hold values from -0.0625 to 0.0625
- seq_ids: int32 [4096], P('dp'), may hold values from 0 to 127, as said below
Outputs:
- eig_scale: float32 [4096, 4096], P(('blk', 'pair'), 'dp')
Inputs may be any that keep to these rules, and one draw needn't show every extreme that they name: seq_ids never fall along the tokens; the 128 tokens of index k of dp carry exactly the ids k * 4 to k * 4 + 3, each at least once.
All inputs are finite; a program needn't handle non-finite values.
Results may differ from a plain program's by a relative error of at most 0.0017.
Values may be sent and summed in bfloat16 or wider, within the bound.
A program may use at most 64 MiB of HBM per device.

v0:
```python
import jax
import jax.numpy as jnp
from jax import lax
from jax.sharding import PartitionSpec as P

SEQ_DEV = 4


def square_block(masked, piece):
    per_seq = jnp.einsum("sti,tj->sij", masked, piece, preferred_element_type=jnp.float32)
    return jnp.sum(per_seq * per_seq, axis=0)


def on_device(acts, grads, basis_in, basis_out, seq_ids):
    moved_in, moved_out = (
        lax.all_to_all(acts, "dp", split_axis=1, concat_axis=0, tiled=True),
        lax.all_to_all(grads, "dp", split_axis=1, concat_axis=0, tiled=True),
    )
    part_in = jnp.dot(
        moved_in, basis_in, precision=lax.Precision.HIGHEST, preferred_element_type=jnp.float32
    )
    part_out = jnp.dot(
        moved_out, basis_out, precision=lax.Precision.HIGHEST, preferred_element_type=jnp.float32
    )
    part_in = part_in.astype(jnp.bfloat16)[:, None, :]
    part_out = part_out.astype(jnp.bfloat16)[:, None, :]
    recv_in, recv_out = (
        lax.all_to_all(part_in, "dp", split_axis=0, concat_axis=1, tiled=True),
        lax.all_to_all(part_out, "dp", split_axis=0, concat_axis=1, tiled=True),
    )
    rot_in = jnp.sum(recv_in.astype(jnp.float32), axis=1).astype(jnp.bfloat16)
    rot_out = jnp.sum(recv_out.astype(jnp.float32), axis=1).astype(jnp.bfloat16)
    slots = seq_ids % SEQ_DEV
    member = slots[None, :] == jnp.arange(SEQ_DEV, dtype=jnp.int32)[:, None]
    masked = jnp.where(member[:, :, None], rot_out[None, :, :], jnp.zeros((), jnp.bfloat16))
    squared = square_block(masked, lax.all_gather(rot_in, ("blk", "pair"), axis=1, tiled=True))
    groups = lax.axis_size("dp")
    partial_value = squared / jnp.float32(SEQ_DEV * groups)
    return lax.psum_scatter(partial_value, "dp", scatter_dimension=1, tiled=True)


def solution(mesh):
    return jax.shard_map(
        on_device,
        mesh=mesh,
        in_specs=(
            P("dp", None),
            P("dp", None),
            P("dp", ("blk", "pair")),
            P("dp", ("blk", "pair")),
            P("dp"),
        ),
        out_specs=P(("blk", "pair"), "dp"),
        check_vma=False,
    )
```

profile of v0, /device:TPU:6, one launch (start us, length us, event | category | flops | bytes accessed | tf_op | source)
XLA Modules:
  0.0 1128.3 jit_solution(2848925855283160429)
XLA Ops:
  6.5 0.0 copy-start
  6.5 4.1 copy.21
  10.7 18.1 %all-to-all-start.2 = ((bf16[128,32,256]{0,2,1:T(8,128)(2,1)}), bf16[128,32,256]{0,2,1:T(8,128)(2,1)S(1)}, u32[]{:S(2)}, u32[]{:S(2)}) async-start(bf16[128,32,256]{0,2,1:T(8,128)(2,1)} %bitcast.24), calls=%async_computation.2 | async-start | bytes 4194304 | tf_op jit(solution)/shard_map/all_to_all | solution.py:16
  28.8 4.1 copy.17
  32.9 91.7 %all-to-all-done.2 = bf16[128,32,256]{0,2,1:T(8,128)(2,1)S(1)} async-done(((bf16[128,32,256]{0,2,1:T(8,128)(2,1)}), bf16[128,32,256]{0,2,1:T(8,128)(2,1)S(1)}, u32[]{:S(2)}, u32[]{:S(2)}) %all-to-all-start.2) | async-done | bytes 2097184 | tf_op jit(solution)/shard_map/all_to_all | solution.py:16
  124.6 0.0 copy-start.3
  124.6 1.3 copy-done.3
  125.9 9.6 all-to-all-start
  135.5 4.1 copy.22
  139.5 0.0 copy-done
  139.6 4.7 fusion.1
  144.3 0.5 broadcast.20
  144.8 4.5 reduce.8
  149.3 4.0 reshape.28
  153.3 77.8 %all-to-all-done = bf16[128,32,256]{0,2,1:T(8,128)(2,1)S(1)} async-done(((bf16[128,32,256]{0,2,1:T(8,128)(2,1)}), bf16[128,32,256]{0,2,1:T(8,128)(2,1)S(1)}, u32[]{:S(2)}, u32[]{:S(2)}) %all-to-all-start) | async-done | bytes 2097184 | tf_op jit(solution)/shard_map/all_to_all | solution.py:17
  231.1 0.0 copy-start.2
  231.1 1.3 copy-done.2
  232.4 9.6 all-to-all-start.3
  242.0 0.0 copy-start.4
  242.0 4.1 copy.18
  246.1 0.0 copy-done.4
  246.1 4.7 fusion
  250.9 4.5 reduce.9
  255.4 4.0 reshape.30
  259.3 78.5 %all-to-all-done.3 = bf16[32,2,16384]{2,1,0:T(2,128)(2,1)S(1)} async-done(((bf16[32,2,16384]{2,1,0:T(2,128)(2,1)}), bf16[32,2,16384]{2,1,0:T(2,128)(2,1)S(1)}, u32[]{:S(2)}, u32[]{:S(2)}) %all-to-all-start.3) | async-done | bytes 2097184 | tf_op jit(solution)/shard_map/all_to_all | solution.py:28
  337.8 0.0 copy-start.1
  337.8 1.3 copy-done.1
  339.2 9.6 all-to-all-start.1
  348.8 0.0 all-gather.2.cloned.1.call-start
  348.8 10.4 reshape.29
  359.3 3.9 copy.25
  363.1 0.0 copy-start.5
  363.1 2.5 reduce_sum.34
  365.7 0.0 all-gather.2.cloned.1.call-update
  365.7 0.2 reduce-scatter.2.cloned.1.call-start
  365.9 0.0 copy-done.5
  366.0 78.6 %all-to-all-done.1 = bf16[32,2,16384]{2,1,0:T(2,128)(2,1)S(1)} async-done(((bf16[32,2,16384]{2,1,0:T(2,128)(2,1)}), bf16[32,2,16384]{2,1,0:T(2,128)(2,1)S(1)}, u32[]{:S(2)}, u32[]{:S(2)}) %all-to-all-start.1) | async-done | bytes 2097184 | tf_op jit(solution)/shard_map/all_to_all | solution.py:29
  444.5 6.8 reshape.31
  451.3 2.5 copy.24
  453.8 0.3 reduce_sum.33
  454.1 0.1 copy.20
  454.2 0.0 all-gather.2.cloned.1.call-done
  454.3 3.9 multiply_reduce_fusion
  458.2 2.3 broadcast_multiply_fusion
  460.6 0.0 reduce-scatter.2.cloned.1.call-update
  460.6 660.9 %reduce-scatter.2.cloned.1.call-done = f32[256,128]{1,0:T(8,128)} async-done(((f32[256,4096]{1,0:T(8,128)}), f32[256,128]{1,0:T(8,128)}) %reduce-scatter.2.cloned.1.call-update) | async-done | bytes 131088 | tf_op jit(solution)/shard_map/reduce_scatter | solution.py:39
  (2 shorter events, 0.0 us)
Async XLA Ops:
  6.5 133.0 %copy-start = (f32[256,256]{1,0:T(8,128)S(1)}, f32[256,256]{1,0:T(8,128)}, u32[]{:S(2)}) copy-start(f32[256,256]{1,0:T(8,128)} %param.7) | copy-start | bytes 786436
  10.7 113.9 %all-to-all-start.2 = ((bf16[128,32,256]{0,2,1:T(8,128)(2,1)}), bf16[128,32,256]{0,2,1:T(8,128)(2,1)S(1)}, u32[]{:S(2)}, u32[]{:S(2)}) async-start(bf16[128,32,256]{0,2,1:T(8,128)(2,1)} %bitcast.24), calls=%async_computation.2 | async-start | bytes 4194304 | tf_op jit(solution)/shard_map/all_to_all | solution.py:16
  124.6 1.3 copy-start.3
  125.9 105.2 %all-to-all-start = ((bf16[128,32,256]{0,2,1:T(8,128)(2,1)}), bf16[128,32,256]{0,2,1:T(8,128)(2,1)S(1)}, u32[]{:S(2)}, u32[]{:S(2)}) async-start(bf16[128,32,256]{0,2,1:T(8,128)(2,1)} %bitcast.22), calls=%async_computation | async-start | bytes 4194304 | tf_op jit(solution)/shard_map/all_to_all | solution.py:17
  231.1 1.3 copy-start.2
  232.4 105.4 %all-to-all-start.3 = ((bf16[32,2,16384]{2,1,0:T(2,128)(2,1)}), bf16[32,2,16384]{2,1,0:T(2,128)(2,1)S(1)}, u32[]{:S(2)}, u32[]{:S(2)}) async-start(bf16[32,2,16384]{2,1,0:T(2,128)(2,1)} %reshape.28), calls=%async_computation.3 | async-start | bytes 4194304 | tf_op jit(solution)/shard_map/all_to_all | solution.py:28
  242.0 4.1 copy-start.4
  337.8 1.3 copy-start.1
  339.2 105.3 %all-to-all-start.1 = ((bf16[32,2,16384]{2,1,0:T(2,128)(2,1)}), bf16[32,2,16384]{2,1,0:T(2,128)(2,1)S(1)}, u32[]{:S(2)}, u32[]{:S(2)}) async-start(bf16[32,2,16384]{2,1,0:T(2,128)(2,1)} %reshape.30), calls=%async_computation.1 | async-start | bytes 4194304 | tf_op jit(solution)/shard_map/all_to_all | solution.py:29
  348.8 105.5 %all-gather.2.cloned.1.call-start = ((), (), s32[]{:S(2)}) async-start(), calls=%async_computation.5 | async-start | bytes 1114112 | tf_op jit(solution)/shard_map/all_gather | solution.py:36
  363.1 2.8 copy-start.5
  365.7 755.8 %reduce-scatter.2.cloned.1.call-start = ((), (), s32[]{:S(2)}) async-start(), calls=%async_computation.6 | async-start | bytes 4325376 | tf_op jit(solution)/shard_map/reduce_scatter | solution.py:39
Sparse Core Ops, SparseCore 0:
  365.8 49.3 all-gather.1
  460.7 660.7 reduce-scatter.1
where the time goes:
time: 1130 us
  waiting for transfers between devices  988 us (87%)
  local copies, waits for them, and re-layouts  52.5 us (5%)
  starting transfers between devices  47.1 us (4%)
  other arithmetic  14.2 us (1%)
  between operations  13.5 us (1%)
  matrix products  13.4 us (1%)
    reduce_scatter x1, waiting for transfers between devices, on_device(): lax.psum_scatter(partial_value, 'dp', scatter_dimension=1, tiled=True)  661 us
    all_to_all x1, waiting for transfers between devices, on_device(): lax.all_to_all(acts, 'dp', split_axis=1, concat_axis=0, tiled=True)  91.7 us
    all_to_all x1, waiting for transfers between devices, on_device(): lax.all_to_all(part_out, 'dp', split_axis=0, concat_axis=1, tiled=True)  78.6 us
    all_to_all x1, waiting for transfers between devices, on_device(): lax.all_to_all(part_in, 'dp', split_axis=0, concat_axis=1, tiled=True)  78.5 us
    all_to_all x1, waiting for transfers between devices, on_device(): lax.all_to_all(grads, 'dp', split_axis=1, concat_axis=0, tiled=True)  77.8 us
    unnamed x20, local copies, waits for them, and re-layouts  43.7 us
  transfers between devices with their start and end apart: 6, of which 5 were waited for; matrix products, arithmetic and copies ran while one was open for 6% of the time, Pallas kernels for 0%

commit v1 on v0

v1 whole, which is shorter than its diff:
```python
import jax
import jax.numpy as jnp
from jax import lax
from jax.experimental import pallas as pl
from jax.experimental.pallas import tpu as pltpu
from jax.sharding import PartitionSpec as P

SEQ_DEV = 4
TOK = 128
NZ = 16
NH = 2
COLS = 256
ROWS = 256
HALF = NZ * ROWS
TAG = 16
MESH = pl.DeviceIdType.MESH
F32 = jnp.float32
BF16 = jnp.bfloat16


class Ring:
    hops = ((8, 7), (7, 8))

    def __init__(self, buf, cuts, send, recv, h, z):
        self.buf, self.cuts, self.send, self.recv, self.h, self.z = buf, cuts, send, recv, h, z

    def copy(self, way, part, t, origin):
        sign = 1 if way == 0 else -1
        low, size = self.cuts[part]
        piece = self.buf.at[origin, pl.ds(low, size)]
        return pltpu.make_async_remote_copy(
            src_ref=piece, dst_ref=piece,
            send_sem=self.send.at[way, part, t], recv_sem=self.recv.at[way, part, t],
            device_id={"dp": self.h * NZ + lax.rem(self.z + sign + NZ, NZ)}, device_id_type=MESH)

    def slot(self, way, t):
        sign = 1 if way == 0 else -1
        return lax.rem(self.z - sign * t + NZ, NZ)

    def step(self, s):
        for part in range(2):
            for way in range(2):
                hops = self.hops[way][part]
                if 1 <= s <= hops:
                    self.copy(way, part, s - 1, self.slot(way, s)).wait_recv()
                if s < hops:
                    self.copy(way, part, s, self.slot(way, s)).start()

    def slots(self, s):
        if s == 0:
            return [self.z]
        if s == NZ // 2:
            return [self.slot(0, s)]
        return [self.slot(0, s), self.slot(1, s)]

    def finish(self):
        for part in range(2):
            for way in range(2):
                for t in range(self.hops[way][part]):
                    self.copy(way, part, t, self.slot(way, t)).wait_send()


def kernel(acts, grads, basis_in, basis_out, seq, out,
           a_in, a_out, b_in, b_out, f_in, f_out, acc, psend, precv, rots, gath, right, osum, orecv,
           load, in_s, in_r, out_s, out_r, g_s, g_r, y_s, y_r, k_s, k_r, h_s, h_r, p_s, p_r, q_s, q_r, t_s, t_r):
    blk, pair, dp = lax.axis_index("blk"), lax.axis_index("pair"), lax.axis_index("dp")
    x, core = blk // 2, lax.rem(blk, 2)
    h, z = dp // NZ, lax.rem(dp, NZ)
    c = blk * 2 + pair
    zc = lax.rem(lax.rem(c, 8) + 7, 8) * 2 + c // 8
    cz = lax.rem(z // 2 + 1, 8) + 8 * lax.rem(z, 2)
    row0 = pl.multiple_of(core * 64, 64)
    other0 = pl.multiple_of((1 - core) * 64, 64)

    across = {"pair": 1 - pair, "dp": (1 - h) * NZ + z}
    twin = {"dp": (1 - h) * NZ + z}
    sibling = {"blk": x * 2 + 1 - core}
    peers = [(dx, dy) for dx in range(4) for dy in range(2) if (dx, dy) != (0, 0)]

    def peer(dx, dy):
        return {"blk": lax.rem(x + dx, 4) * 2 + core, "pair": lax.rem(pair + dy, 2)}

    def collected(dx, dy, k):
        of = (lax.rem(x - dx + 4, 4) * 2 + k) * 2 + lax.rem(pair + dy, 2)
        return lax.rem(lax.rem(of, 8) + 7, 8) * 2 + of // 8

    mine = pl.ds(pl.multiple_of(h * HALF, HALF), HALF)
    theirs = pl.ds(pl.multiple_of((1 - h) * HALF, HALF), HALF)
    loads = [
        pltpu.make_async_copy(basis_in, f_in, load.at[0]),
        pltpu.make_async_copy(basis_out, f_out, load.at[1]),
        pltpu.make_async_copy(acts.at[:, mine], a_in.at[pl.ds(0, TOK)], load.at[2]),
        pltpu.make_async_copy(grads.at[:, mine], a_out.at[pl.ds(0, TOK)], load.at[3]),
    ]
    for one in loads:
        one.start()

    barrier = pltpu.get_barrier_semaphore()
    greet = [
        {"dp": h * NZ + lax.rem(z + 1, NZ)},
        {"dp": h * NZ + lax.rem(z + NZ - 1, NZ)},
        across, twin, sibling,
        {"blk": (z // 2) // 2, "pair": lax.rem(z // 2, 2), "dp": h * NZ + zc},
        {"blk": (z // 2) // 2 + 4, "pair": lax.rem(z // 2, 2), "dp": h * NZ + zc},
    ] + [peer(dx, dy) for dx, dy in peers]
    for device in greet:
        pl.semaphore_signal(barrier, inc=1, device_id=device, device_id_type=MESH)

    loads[0].wait()
    b_in[z] = f_in[...].astype(BF16)
    loads[1].wait()
    b_out[z] = f_out[...].astype(BF16)
    tags = jnp.bitwise_and(seq[...], SEQ_DEV - 1).astype(F32)
    gath[z, COLS:COLS + TAG] = jnp.broadcast_to(tags, (TAG, TOK)).astype(BF16)
    osum[...] = jnp.zeros_like(osum)
    acc[...] = jnp.zeros_like(acc)

    pl.semaphore_wait(barrier, len(greet))

    halves = ((0, ROWS // 2), (ROWS // 2, ROWS // 2))
    ring_in = Ring(b_in, halves, in_s, in_r, h, z)
    ring_out = Ring(b_out, halves, out_s, out_r, h, z)
    ring_g = Ring(gath, ((0, 144), (144, 128)), g_s, g_r, h, z)

    def y_copy(i):
        source, held = ((acts, a_in), (grads, a_out))[i]
        return pltpu.make_async_remote_copy(
            src_ref=source.at[pl.ds(row0, 64), theirs], dst_ref=held.at[pl.ds(TOK + row0, 64)],
            send_sem=y_s.at[i], recv_sem=y_r.at[i], device_id=across, device_id_type=MESH)

    def k_copy(i, first):
        piece = (a_in, a_out)[i].at[pl.ds(TOK + first, 64)]
        return pltpu.make_async_remote_copy(
            src_ref=piece, dst_ref=piece, send_sem=k_s.at[i], recv_sem=k_r.at[i],
            device_id=sibling, device_id_type=MESH)

    def h_copy(i):
        return pltpu.make_async_remote_copy(
            src_ref=psend.at[i], dst_ref=precv.at[i], send_sem=h_s.at[i], recv_sem=h_r.at[i],
            device_id=twin, device_id_type=MESH)

    def p_copy(q):
        return pltpu.make_async_remote_copy(
            src_ref=rots.at[q], dst_ref=right.at[z, c // 8], send_sem=p_s.at[q], recv_sem=p_r.at[c // 8],
            device_id={"blk": cz // 2, "pair": lax.rem(cz, 2), "dp": h * NZ + 2 * lax.rem(c, 8) + q},
            device_id_type=MESH)

    def p_arrive(j):
        piece = right.at[zc, j]
        pltpu.make_async_remote_copy(
            src_ref=piece, dst_ref=piece, send_sem=p_s.at[0], recv_sem=p_r.at[j],
            device_id=twin, device_id_type=MESH).wait_recv()

    def q_copy(n, block):
        piece = right.at[block]
        return pltpu.make_async_remote_copy(
            src_ref=piece, dst_ref=piece, send_sem=q_s.at[n], recv_sem=q_r.at[n],
            device_id=peer(*peers[n]), device_id_type=MESH)

    def t_copy(n, block):
        piece = right.at[block]
        return pltpu.make_async_remote_copy(
            src_ref=piece, dst_ref=piece, send_sem=t_s.at[n], recv_sem=t_r.at[n],
            device_id=sibling, device_id_type=MESH)

    def add_block(i, slot):
        held, basis = ((a_in, b_in), (a_out, b_out))[i]
        columns = pl.ds(pl.multiple_of(slot * ROWS, ROWS), ROWS)
        acc[i] += jnp.dot(held[:, columns], basis[slot], preferred_element_type=F32)

    def square(slot):
        left = gath[slot, 0:COLS]
        ids = gath[slot, COLS:COLS + TAG].astype(F32)[0:1]
        block = jnp.concatenate([right[slot, 0], right[slot, 1]], axis=1)
        total = None
        for s in range(SEQ_DEV):
            member = jnp.where(ids == F32(s), F32(1), F32(0)).astype(BF16)
            product = jnp.dot(left * member, block, preferred_element_type=F32)
            product = product * product
            total = product if total is None else total + product
        osum[0] += total[:, :TOK]
        osum[1] += total[:, TOK:]

    ring_in.step(0)
    y_copy(0).start()
    for s in range(1, 9):
        if s == 8:
            ring_out.step(0)
        ring_in.step(s)
        if s == 5:
            y_copy(0).wait_recv()
            k_copy(0, row0).start()
            y_copy(1).start()
    loads[2].wait()
    k_copy(0, other0).wait_recv()
    ring_out.step(1)

    @pl.loop(0, NZ)
    def _(slot):
        add_block(0, slot)

    psend[0] = acc[0, TOK:].astype(BF16)
    h_copy(0).start()

    for s in range(2, 9):
        ring_out.step(s)
        if s == 2:
            h_copy(0).wait_recv()
            rotated = (acc[0, :TOK] + precv[0].astype(F32)).astype(BF16)
            rots[0] = rotated[:, :TOK]
            rots[1] = rotated[:, TOK:]
            for q in range(2):
                p_copy(q).start()
            y_copy(1).wait_recv()
            k_copy(1, row0).start()
        if s == 3:
            for j in range(2):
                p_arrive(j)
            for n in range(len(peers)):
                q_copy(n, zc).start()
            t_copy(7, zc).start()
        if s == 4:
            loads[3].wait()
            k_copy(1, other0).wait_recv()

            @pl.loop(0, 2 * s + 1)
            def _(i):
                add_block(1, lax.rem(z + NZ - 4 + i, NZ))
        if s > 4:
            for slot in ring_out.slots(s):
                add_block(1, slot)
        if s == 6:
            for n, (dx, dy) in enumerate(peers):
                block = collected(dx, dy, core)
                q_copy(n, block).wait_recv()
                t_copy(n, block).start()

    psend[1] = acc[1, TOK:].astype(BF16)
    h_copy(1).start()
    for n, (dx, dy) in enumerate(peers):
        t_copy(n, collected(dx, dy, 1 - core)).wait_recv()
    t_copy(7, collected(0, 0, 1 - core)).wait_recv()
    h_copy(1).wait_recv()
    rotated = acc[1, :TOK] + precv[1].astype(F32)
    gath[z, 0:COLS] = rotated.T.astype(BF16)

    for s in range(9):
        ring_g.step(s)
        for slot in ring_g.slots(s):
            square(slot)

    last = pltpu.make_async_remote_copy(
        src_ref=osum.at[1 - h], dst_ref=orecv, send_sem=h_s.at[2], recv_sem=h_r.at[2],
        device_id=twin, device_id_type=MESH)
    last.start()

    ring_in.finish()
    ring_out.finish()
    ring_g.finish()
    for i in range(2):
        y_copy(i).wait_send()
        k_copy(i, row0).wait_send()
        h_copy(i).wait_send()
        p_copy(i).wait_send()
    for n, (dx, dy) in enumerate(peers):
        q_copy(n, zc).wait_send()
        t_copy(n, collected(dx, dy, core)).wait_send()
    t_copy(7, zc).wait_send()

    last.wait_recv()
    out[...] = (osum[h] + orecv[...]) * F32(1.0 / (SEQ_DEV * NZ * NH))
    last.wait_send()


def on_device(acts, grads, basis_in, basis_out, seq_ids):
    dma = pltpu.SemaphoreType.DMA
    ring = dma((2, 2, 8))
    return pl.pallas_call(
        kernel,
        out_shape=jax.ShapeDtypeStruct((COLS, TOK), F32),
        in_specs=[pl.BlockSpec(memory_space=pl.ANY)] * 4 + [pl.BlockSpec(memory_space=pltpu.VMEM)],
        out_specs=pl.BlockSpec(memory_space=pltpu.VMEM),
        scratch_shapes=[
            pltpu.VMEM((NH * TOK, HALF), BF16),
            pltpu.VMEM((NH * TOK, HALF), BF16),
            pltpu.VMEM((NZ, ROWS, COLS), BF16),
            pltpu.VMEM((NZ, ROWS, COLS), BF16),
            pltpu.VMEM((ROWS, COLS), F32),
            pltpu.VMEM((ROWS, COLS), F32),
            pltpu.VMEM((2, NH * TOK, COLS), F32),
            pltpu.VMEM((2, TOK, COLS), BF16),
            pltpu.VMEM((2, TOK, COLS), BF16),
            pltpu.VMEM((2, TOK, TOK), BF16),
            pltpu.VMEM((NZ, COLS + TAG, TOK), BF16),
            pltpu.VMEM((NZ, NH, TOK, TOK), BF16),
            pltpu.VMEM((NH, COLS, TOK), F32),
            pltpu.VMEM((COLS, TOK), F32),
            dma((4,)),
            ring, ring, ring, ring, ring, ring,
            dma((2,)), dma((2,)), dma((2,)), dma((2,)), dma((3,)), dma((3,)),
            dma((2,)), dma((2,)), dma((7,)), dma((7,)), dma((8,)), dma((8,)),
        ],
        compiler_params=pltpu.CompilerParams(
            collective_id=0, has_side_effects=True, vmem_limit_bytes=40 * 1024 * 1024),
        cost_estimate=pl.CostEstimate(flops=3_300_000_000, bytes_accessed=8_000_000, transcendentals=0),
    )(acts, grads, basis_in, basis_out, seq_ids.reshape(1, TOK))


def solution(mesh):
    return jax.shard_map(
        on_device,
        mesh=mesh,
        in_specs=(
            P("dp", None),
            P("dp", None),
            P("dp", ("blk", "pair")),
            P("dp", ("blk", "pair")),
            P("dp"),
        ),
        out_specs=P(("blk", "pair"), "dp"),
        check_vma=False,
    )
```

time: 1130 us -> 131 us (0.12)
  waiting for transfers between devices: 988 us -> 0 us
  Pallas kernels: 0 us -> 122 us
  starting transfers between devices: 47.1 us -> 0 us
  local copies, waits for them, and re-layouts: 52.5 us -> 6.39 us
  other arithmetic: 14.2 us -> 0 us
  between operations: 13.5 us -> 0.01 us
  matrix products: 13.4 us -> 0 us
    reduce_scatter x1 -> x0, waiting for transfers between devices: 661 us -> none  [on_device(): lax.psum_scatter(partial_value, 'dp', scatter_dimension=1, tiled=True)]
    all_to_all x4 -> x0, waiting for transfers between devices: 327 us -> none  [the longest x1 91.7 us: on_device(): lax.all_to_all(acts, 'dp', split_axis=1, concat_axis=0, tiled=True)]
    pallas_call x0 -> x1, Pallas kernels: none -> 122 us  [on_device(): pl.pallas_call(kernel, out_shape=jax.ShapeDtypeStruct((COLS, TOK), F32),...]
    all_to_all x4 -> x0, starting transfers between devices: 46.9 us -> none  [the longest x1 18.1 us: on_device(): lax.all_to_all(acts, 'dp', split_axis=1, concat_axis=0, tiled=True)]
    unnamed x20 -> x11, local copies, waits for them, and re-layouts: 43.7 us -> 6.39 us
    dot_general x3 -> x0, matrix products: 13.4 us -> none  [the longest x1 4.74 us: on_device(): jnp.dot(moved_in, basis_in, precision=lax.Precision.HIGHEST, preferred_el...]
  transfers between devices with their start and end apart: 6 -> 0, of which waited for: 5 -> 0; matrix products, arithmetic and copies ran while one was open for 6% -> 0% of each run, Pallas kernels for 0% -> 0%
where the time goes in v1:
time: 131 us; the launch traced here: 129 us
  Pallas kernels  122 us (93%)
  local copies, waits for them, and re-layouts  6.39 us (5%)
    pallas_call x1, Pallas kernels, on_device(): pl.pallas_call(kernel, out_shape=jax.ShapeDtypeStruct((COLS, TOK), F32),...  122 us
    unnamed x11, local copies, waits for them, and re-layouts  6.39 us

profile of v1, /device:TPU:6, one launch (start us, length us, event | category | flops | bytes accessed | tf_op | source)
XLA Modules:
  0.0 128.7 jit_solution(18025702966182175968)
XLA Ops:
  0.0 0.0 copy-start
  0.0 1.6 %copy-done = bf16[128,8192]{1,0:T(8,128)(2,1)S(1)} copy-done((bf16[128,8192]{1,0:T(8,128)(2,1)S(1)}, bf16[128,8192]{1,0:T(8,128)(2,1)}, u32[]{:S(2)}) %copy-start) | copy-done | bytes 2097176
  1.6 0.0 copy-start.1
  1.6 1.6 %copy-done.1 = bf16[128,8192]{1,0:T(8,128)(2,1)S(1)} copy-done((bf16[128,8192]{1,0:T(8,128)(2,1)S(1)}, bf16[128,8192]{1,0:T(8,128)(2,1)}, u32[]{:S(2)}) %copy-start.1) | copy-done | bytes 2097176
  3.2 0.0 copy-start.2
  3.2 0.9 copy-done.2
  4.1 0.0 copy-start.3
  4.1 0.9 copy-done.3
  5.1 0.0 copy-start.4
  5.1 0.7 copy-done.4
  5.7 122.3 %shard_map.55 = f32[256,128]{1,0:T(8,128)S(1)} custom-call(bf16[128,8192]{1,0:T(8,128)(2,1)S(1)} %copy-done, bf16[128,8192]{1,0:T(8,128)(2,1)S(1)} %copy-done.1, f32[256,256]{1,0:T(8,128)S(1)} %copy-done.2, f32[256,256]{1,0:T(8,128)S(1)} %copy-done.3, s32[1,128]{1,0:T(1,128)S(1)} %bitcast.1), custom_call_target="tpu_custom_call" | custom-call | flops 3300000000 | bytes 8000000 | tf_op jit(solution)/shard_map/pallas_call | solution.py:278
  128.0 0.7 copy.7
Async XLA Ops:
  0.0 1.6 %copy-start = (bf16[128,8192]{1,0:T(8,128)(2,1)S(1)}, bf16[128,8192]{1,0:T(8,128)(2,1)}, u32[]{:S(2)}) copy-start(bf16[128,8192]{1,0:T(8,128)(2,1)} %acts.1) | copy-start | bytes 6291460
  1.6 1.6 %copy-start.1 = (bf16[128,8192]{1,0:T(8,128)(2,1)S(1)}, bf16[128,8192]{1,0:T(8,128)(2,1)}, u32[]{:S(2)}) copy-start(bf16[128,8192]{1,0:T(8,128)(2,1)} %grads.1) | copy-start | bytes 6291460
  3.2 0.9 copy-start.2
  4.1 0.9 copy-start.3
  5.1 0.7 copy-start.4

commit v2 on v1

--- a/solution.py
+++ b/solution.py
@@ -12,6 +12,7 @@
 COLS = 256
 ROWS = 256
 HALF = NZ * ROWS
+LAG = 4
 TAG = 16
 MESH = pl.DeviceIdType.MESH
 F32 = jnp.float32
@@ -181,59 +182,63 @@
         osum[0] += total[:, :TOK]
         osum[1] += total[:, TOK:]
 
-    ring_in.step(0)
-    y_copy(0).start()
-    for s in range(1, 9):
-        if s == 8:
-            ring_out.step(0)
-        ring_in.step(s)
-        if s == 5:
+    def add_blocks(i, near, far):
+        @pl.loop(2 * near, 2 * far + 2)
+        def _(n):
+            add_block(i, lax.rem(z + NZ + (2 * lax.rem(n, 2) - 1) * (n // 2), NZ))
+
+    for m in range(LAG + 9):
+        if m <= 8:
+            ring_in.step(m)
+        if m >= LAG:
+            ring_out.step(m - LAG)
+        if m == 0:
+            y_copy(0).start()
+        if m == 4:
             y_copy(0).wait_recv()
             k_copy(0, row0).start()
             y_copy(1).start()
-    loads[2].wait()
-    k_copy(0, other0).wait_recv()
-    ring_out.step(1)
-
-    @pl.loop(0, NZ)
-    def _(slot):
-        add_block(0, slot)
-
-    psend[0] = acc[0, TOK:].astype(BF16)
-    h_copy(0).start()
-
-    for s in range(2, 9):
-        ring_out.step(s)
-        if s == 2:
+        if m == 5:
+            loads[2].wait()
+            k_copy(0, other0).wait_recv()
+            add_block(0, z)
+            add_blocks(0, 1, 2)
+        if m == 6:
+            add_blocks(0, 3, 4)
+        if m == 7:
+            add_blocks(0, 5, 7)
+            y_copy(1).wait_recv()
+            k_copy(1, row0).start()
+        if m == 8:
+            add_block(0, ring_in.slots(8)[0])
+            psend[0] = acc[0, TOK:].astype(BF16)
+            h_copy(0).start()
+        if m == 9:
             h_copy(0).wait_recv()
             rotated = (acc[0, :TOK] + precv[0].astype(F32)).astype(BF16)
             rots[0] = rotated[:, :TOK]
             rots[1] = rotated[:, TOK:]
             for q in range(2):
                 p_copy(q).start()
-            y_copy(1).wait_recv()
-            k_copy(1, row0).start()
-        if s == 3:
+            loads[3].wait()
+            k_copy(1, other0).wait_recv()
+            add_block(1, z)
+            add_blocks(1, 1, 2)
+        if m == 10:
             for j in range(2):
                 p_arrive(j)
             for n in range(len(peers)):
                 q_copy(n, zc).start()
             t_copy(7, zc).start()
-        if s == 4:
-            loads[3].wait()
-            k_copy(1, other0).wait_recv()
-
-            @pl.loop(0, 2 * s + 1)
-            def _(i):
-                add_block(1, lax.rem(z + NZ - 4 + i, NZ))
-        if s > 4:
-            for slot in ring_out.slots(s):
-                add_block(1, slot)
-        if s == 6:
+            add_blocks(1, 3, 5)
+        if m == 11:
             for n, (dx, dy) in enumerate(peers):
                 block = collected(dx, dy, core)
                 q_copy(n, block).wait_recv()
                 t_copy(n, block).start()
+            add_blocks(1, 6, 7)
+        if m == 12:
+            add_block(1, ring_out.slots(8)[0])
 
     psend[1] = acc[1, TOK:].astype(BF16)
     h_copy(1).start()
@@ -301,7 +306,7 @@
             dma((2,)), dma((2,)), dma((7,)), dma((7,)), dma((8,)), dma((8,)),
         ],
         compiler_params=pltpu.CompilerParams(
-            collective_id=0, has_side_effects=True, vmem_limit_bytes=40 * 1024 * 1024),
+            collective_id=0, has_side_effects=True, vmem_limit_bytes=62 * 1024 * 1024),
         cost_estimate=pl.CostEstimate(flops=3_300_000_000, bytes_accessed=8_000_000, transcendentals=0),
     )(acts, grads, basis_in, basis_out, seq_ids.reshape(1, TOK))
 

time: 131 us -> 121 us (0.924)
  the two profiles are of different devices: /device:TPU:6 before, /device:TPU:8 now
where the time goes in v2:
time: 121 us
  Pallas kernels  119 us (98%)
  local copies, waits for them, and re-layouts  1.57 us (1%)
    pallas_call x1, Pallas kernels, on_device(): pl.pallas_call(kernel, out_shape=jax.ShapeDtypeStruct((COLS, TOK), F32),...  119 us

profile of v2, /device:TPU:8, one launch (start us, length us, event | category | flops | bytes accessed | tf_op | source)
XLA Modules:
  0.0 121.0 jit_solution(8471222356375377494)
XLA Ops:
  0.0 119.5 %shard_map.55 = f32[256,128]{1,0:T(8,128)} custom-call(bf16[128,8192]{1,0:T(8,128)(2,1)} %acts.1, bf16[128,8192]{1,0:T(8,128)(2,1)} %grads.1, f32[256,256]{1,0:T(8,128)} %basis_in.1, f32[256,256]{1,0:T(8,128)} %basis_out.1, s32[1,128]{1,0:T(1,128)} %bitcast.1), custom_call_target="tpu_custom_call" | custom-call | flops 3300000000 | bytes 8000000 | tf_op jit(solution)/shard_map/pallas_call | solution.py:283
  119.5 1.6 %copy.7 = f32[256,128]{1,0:T(8,128)} copy(f32[256,128]{1,0:T(8,128)} %shard_map.55) | data formatting | bytes 262144

commit v3 on v2

v3 whole, which is shorter than its diff:
```python
import jax
import jax.numpy as jnp
from jax import lax
from jax.experimental import pallas as pl
from jax.experimental.pallas import tpu as pltpu
from jax.sharding import PartitionSpec as P

SEQ_DEV = 4
TOK = 128
NZ = 16
NH = 2
COLS = 256
ROWS = 256
HALF = NZ * ROWS
LAG_A = 2
LAG_B = 5
TAG = 16
MESH = pl.DeviceIdType.MESH
F32 = jnp.float32
BF16 = jnp.bfloat16


class Ring:
    def __init__(self, piece, hops, send, recv, h, z):
        self.piece, self.hops, self.send, self.recv, self.h, self.z = piece, hops, send, recv, h, z

    def slot(self, way, t):
        return lax.rem(self.z + (NZ - t if way == 0 else t), NZ)

    def copy(self, way, part, t, origin):
        piece = self.piece(part, origin)
        return pltpu.make_async_remote_copy(
            src_ref=piece, dst_ref=piece,
            send_sem=self.send.at[way, part, t], recv_sem=self.recv.at[way, part, t],
            device_id={"dp": self.h * NZ + self.slot(1 - way, 1)}, device_id_type=MESH)

    def step(self, s):
        for part in range(len(self.hops)):
            for way in range(2):
                hops = self.hops[part][way]
                if 1 <= s <= hops:
                    self.copy(way, part, s - 1, self.slot(way, s)).wait_recv()
                if s < hops:
                    self.copy(way, part, s, self.slot(way, s)).start()

    def finish(self):
        for part in range(len(self.hops)):
            for way in range(2):
                for t in range(self.hops[part][way]):
                    self.copy(way, part, t, self.slot(way, t)).wait_send()


class Skip:
    def __init__(self, piece, hops, send, recv, h, z):
        self.piece, self.hops, self.send, self.recv, self.h, self.z = piece, hops, send, recv, h, z

    def slot(self, way, t):
        return lax.rem(self.z + (NZ - t if way == 0 else t), NZ)

    def copy(self, way, r, far, origin):
        piece = self.piece(origin)
        return pltpu.make_async_remote_copy(
            src_ref=piece, dst_ref=piece,
            send_sem=self.send.at[way, r, far], recv_sem=self.recv.at[way, r, far],
            device_id={"dp": self.h * NZ + self.slot(1 - way, 1 + far)}, device_id_type=MESH)

    def round(self, r):
        for way in range(2):
            if r >= 1 and 2 * r <= self.hops[way]:
                self.copy(way, r - 1, 1, self.slot(way, 2 * r)).wait_recv()
            if r < 4:
                for far in (1, 0):
                    if 2 * r + 1 + far <= self.hops[way]:
                        self.copy(way, r, far, self.slot(way, 2 * r)).start()
        if r >= 1:
            for way in range(2):
                self.copy(way, r - 1, 0, self.slot(way, 2 * r - 1)).wait_recv()

    def slots(self, r):
        if r == 0:
            return [self.z]
        near = [self.slot(0, 2 * r - 1), self.slot(1, 2 * r - 1), self.slot(0, 2 * r)]
        return near if r == 4 else near + [self.slot(1, 2 * r)]

    def finish(self):
        for way in range(2):
            for r in range(4):
                for far in range(2):
                    if 2 * r + 1 + far <= self.hops[way]:
                        self.copy(way, r, far, self.slot(way, 2 * r)).wait_send()


def kernel(acts, grads, basis_in, basis_out, seq, out,
           a_in, a_out, b_in, b_out, f_in, f_out, acc, accs, psend, precv, psends, precvs, rots, gath, gath2, right,
           osum, orecv,
           load, in_s, in_r, out_s, out_r, out2_s, out2_r, g_s, g_r, g2_s, g2_r,
           y_s, y_r, k_s, k_r, h_s, h_r, p_s, p_r, q_s, q_r, t_s, t_r, o_s, o_r):
    blk, pair, dp = lax.axis_index("blk"), lax.axis_index("pair"), lax.axis_index("dp")
    x, core = blk // 2, lax.rem(blk, 2)
    h, z = dp // NZ, lax.rem(dp, NZ)
    c = blk * 2 + pair
    zc = lax.rem(lax.rem(c, 8) + 7, 8) * 2 + c // 8
    cz = lax.rem(z // 2 + 1, 8) + 8 * lax.rem(z, 2)
    row0 = pl.multiple_of(core * 64, 64)
    other0 = pl.multiple_of((1 - core) * 64, 64)

    across = {"pair": 1 - pair, "dp": (1 - h) * NZ + z}
    twin = {"dp": (1 - h) * NZ + z}
    sibling = {"blk": x * 2 + 1 - core}
    peers = [(dx, dy) for dx in range(4) for dy in range(2) if (dx, dy) != (0, 0)]

    def peer(dx, dy):
        return {"blk": lax.rem(x + dx, 4) * 2 + core, "pair": lax.rem(pair + dy, 2)}

    def collected(dx, dy, k):
        of = (lax.rem(x - dx + 4, 4) * 2 + k) * 2 + lax.rem(pair + dy, 2)
        return lax.rem(lax.rem(of, 8) + 7, 8) * 2 + of // 8

    mine = pl.ds(pl.multiple_of(h * HALF, HALF), HALF)
    theirs = pl.ds(pl.multiple_of((1 - h) * HALF, HALF), HALF)
    loads = [
        pltpu.make_async_copy(basis_in, f_in, load.at[0]),
        pltpu.make_async_copy(basis_out, f_out, load.at[1]),
        pltpu.make_async_copy(acts.at[:, mine], a_in.at[pl.ds(0, TOK)], load.at[2]),
        pltpu.make_async_copy(grads.at[:, mine], a_out.at[pl.ds(0, TOK)], load.at[3]),
    ]
    for one in loads:
        one.start()

    barrier = pltpu.get_barrier_semaphore()
    greet = [
        {"dp": h * NZ + lax.rem(z + 1, NZ)},
        {"dp": h * NZ + lax.rem(z + NZ - 1, NZ)},
        {"dp": h * NZ + lax.rem(z + 2, NZ)},
        {"dp": h * NZ + lax.rem(z + NZ - 2, NZ)},
        across, twin, sibling,
        {"blk": (z // 2) // 2, "pair": lax.rem(z // 2, 2), "dp": h * NZ + zc},
        {"blk": (z // 2) // 2 + 4, "pair": lax.rem(z // 2, 2), "dp": h * NZ + zc},
    ] + [peer(dx, dy) for dx, dy in peers]
    for device in greet:
        pl.semaphore_signal(barrier, inc=1, device_id=device, device_id_type=MESH)

    loads[0].wait()
    b_in[z] = f_in[...].astype(BF16)
    loads[1].wait()
    b_out[0, z] = f_out[:, :TOK].astype(BF16)
    b_out[1, z] = f_out[:, TOK:].astype(BF16)
    tags = jnp.bitwise_and(seq[...], SEQ_DEV - 1).astype(F32)
    gath[z, TOK:TOK + TAG] = jnp.broadcast_to(tags, (TAG, TOK)).astype(BF16)
    osum[...] = jnp.zeros_like(osum)
    acc[...] = jnp.zeros_like(acc)
    accs[...] = jnp.zeros_like(accs)

    pl.semaphore_wait(barrier, len(greet))

    part_rows = ROWS // 2
    ring_in = Ring(lambda part, slot: b_in.at[slot, pl.ds(part * part_rows, part_rows)],
                   ((8, 7), (7, 8)), in_s, in_r, h, z)
    ring_a = Ring(lambda part, slot: b_out.at[0, slot], ((8, 7),), out_s, out_r, h, z)
    ring_b = Ring(lambda part, slot: b_out.at[1, slot], ((7, 8),), out2_s, out2_r, h, z)
    ring_ga = Skip(lambda slot: gath.at[slot], (8, 7), g_s, g_r, h, z)
    ring_gb = Skip(lambda slot: gath2.at[slot], (7, 8), g2_s, g2_r, h, z)

    def y_copy(i):
        source, held = ((acts, a_in), (grads, a_out))[i]
        return pltpu.make_async_remote_copy(
            src_ref=source.at[pl.ds(row0, 64), theirs], dst_ref=held.at[pl.ds(TOK + row0, 64)],
            send_sem=y_s.at[i], recv_sem=y_r.at[i], device_id=across, device_id_type=MESH)

    def k_copy(i, first):
        piece = (a_in, a_out)[i].at[pl.ds(TOK + first, 64)]
        return pltpu.make_async_remote_copy(
            src_ref=piece, dst_ref=piece, send_sem=k_s.at[i], recv_sem=k_r.at[i],
            device_id=sibling, device_id_type=MESH)

    def h_copy(i):
        source, target = (psend, precv) if i == 0 else (psends.at[i - 1], precvs.at[i - 1])
        return pltpu.make_async_remote_copy(
            src_ref=source, dst_ref=target, send_sem=h_s.at[i], recv_sem=h_r.at[i],
            device_id=twin, device_id_type=MESH)

    def o_copy(half):
        return pltpu.make_async_remote_copy(
            src_ref=osum.at[half, 1 - h], dst_ref=orecv.at[half], send_sem=o_s.at[half], recv_sem=o_r.at[half],
            device_id=twin, device_id_type=MESH)

    def p_copy(q):
        return pltpu.make_async_remote_copy(
            src_ref=rots.at[q], dst_ref=right.at[z, c // 8], send_sem=p_s.at[q], recv_sem=p_r.at[c // 8],
            device_id={"blk": cz // 2, "pair": lax.rem(cz, 2), "dp": h * NZ + 2 * lax.rem(c, 8) + q},
            device_id_type=MESH)

    def p_arrive(j):
        piece = right.at[zc, j]
        pltpu.make_async_remote_copy(
            src_ref=piece, dst_ref=piece, send_sem=p_s.at[0], recv_sem=p_r.at[j],
            device_id=twin, device_id_type=MESH).wait_recv()

    def q_copy(n, block):
        piece = right.at[block]
        return pltpu.make_async_remote_copy(
            src_ref=piece, dst_ref=piece, send_sem=q_s.at[n], recv_sem=q_r.at[n],
            device_id=peer(*peers[n]), device_id_type=MESH)

    def t_copy(n, block):
        piece = right.at[block]
        return pltpu.make_async_remote_copy(
            src_ref=piece, dst_ref=piece, send_sem=t_s.at[n], recv_sem=t_r.at[n],
            device_id=sibling, device_id_type=MESH)

    def add_in(slot):
        columns = pl.ds(pl.multiple_of(slot * ROWS, ROWS), ROWS)
        acc[...] += jnp.dot(a_in[:, columns], b_in[slot], preferred_element_type=F32)

    def add_out(half, slot):
        columns = pl.ds(pl.multiple_of(slot * ROWS, ROWS), ROWS)
        accs[half] += jnp.dot(a_out[:, columns], b_out[half, slot], preferred_element_type=F32)

    def around(near, far, add):
        @pl.loop(2 * near, 2 * far + 2)
        def _(n):
            add(lax.rem(z + NZ + (2 * lax.rem(n, 2) - 1) * (n // 2), NZ))

    def add_a(slot):
        add_out(0, slot)

    def add_b(slot):
        add_out(1, slot)

    opposite = lax.rem(z + NZ // 2, NZ)

    def square(half, slot):
        left = gath[slot, 0:TOK] if half == 0 else gath2[slot]
        ids = gath[slot, TOK:TOK + TAG].astype(F32)[0:1]
        block = jnp.concatenate([right[slot, 0], right[slot, 1]], axis=1)
        masked = [left * jnp.where(ids == F32(s), F32(1), F32(0)).astype(BF16) for s in range(SEQ_DEV)]
        product = jnp.dot(jnp.concatenate(masked, axis=0), block, preferred_element_type=F32)
        total = None
        for s in range(SEQ_DEV):
            one = product[s * TOK:(s + 1) * TOK]
            total = one * one if total is None else total + one * one
        osum[half, 0] += total[:, :TOK]
        osum[half, 1] += total[:, TOK:]

    def squares(half, r):
        for slot in ring_ga.slots(r):
            square(half, slot)

    def send_partial(half):
        psends[half] = accs[half, TOK:].astype(BF16)
        h_copy(1 + half).start()

    def turned(half):
        h_copy(1 + half).wait_recv()
        return (accs[half, :TOK] + precvs[half].astype(F32)).T.astype(BF16)

    for m in range(LAG_B + 9):
        if m <= 8:
            ring_in.step(m)
        if LAG_A <= m <= LAG_A + 8:
            ring_a.step(m - LAG_A)
        if m >= LAG_B:
            ring_b.step(m - LAG_B)
        if m == 0:
            y_copy(0).start()
            y_copy(1).start()
        if m == 6:
            y_copy(0).wait_recv()
            k_copy(0, row0).start()
        if m == 7:
            loads[2].wait()
            k_copy(0, other0).wait_recv()
            add_in(z)
            around(1, 4, add_in)
            y_copy(1).wait_recv()
            k_copy(1, row0).start()
        if m == 8:
            around(5, 7, add_in)
            add_in(opposite)
            psend[...] = acc[TOK:].astype(BF16)
            h_copy(0).start()
        if m == 9:
            loads[3].wait()
            k_copy(1, other0).wait_recv()
            add_a(z)
            around(1, 6, add_a)
        if m == 10:
            h_copy(0).wait_recv()
            rotated = (acc[:TOK] + precv[...].astype(F32)).astype(BF16)
            rots[0] = rotated[:, :TOK]
            rots[1] = rotated[:, TOK:]
            for q in range(2):
                p_copy(q).start()
            around(7, 7, add_a)
            add_a(opposite)
            send_partial(0)
        if m == 11:
            for j in range(2):
                p_arrive(j)
            for n in range(len(peers)):
                q_copy(n, zc).start()
            t_copy(7, zc).start()
            add_b(z)
            around(1, 5, add_b)
        if m == 12:
            gath[z, 0:TOK] = turned(0)
            ring_ga.round(0)
            for n, (dx, dy) in enumerate(peers):
                block = collected(dx, dy, core)
                q_copy(n, block).wait_recv()
                t_copy(n, block).start()
            around(6, 7, add_b)
        if m == 13:
            add_b(opposite)
            send_partial(1)

    ring_ga.round(1)
    for n, (dx, dy) in enumerate(peers):
        t_copy(n, collected(dx, dy, 1 - core)).wait_recv()
    t_copy(7, collected(0, 0, 1 - core)).wait_recv()
    squares(0, 0)
    squares(0, 1)
    gath2[z] = turned(1)
    ring_gb.round(0)
    ring_ga.round(2)
    squares(1, 0)
    squares(0, 2)
    ring_gb.round(1)
    ring_ga.round(3)
    squares(1, 1)
    squares(0, 3)
    ring_gb.round(2)
    ring_ga.round(4)
    squares(0, 4)
    o_copy(0).start()
    squares(1, 2)
    ring_gb.round(3)
    squares(1, 3)
    ring_gb.round(4)
    squares(1, 4)
    o_copy(1).start()

    for ring in (ring_in, ring_a, ring_b, ring_ga, ring_gb):
        ring.finish()
    for i in range(2):
        y_copy(i).wait_send()
        k_copy(i, row0).wait_send()
        p_copy(i).wait_send()
    for i in range(3):
        h_copy(i).wait_send()
    for n, (dx, dy) in enumerate(peers):
        q_copy(n, zc).wait_send()
        t_copy(n, collected(dx, dy, core)).wait_send()
    t_copy(7, zc).wait_send()

    for half in range(2):
        o_copy(half).wait_recv()
        out[half * TOK:(half + 1) * TOK] = (osum[half, h] + orecv[half]) * F32(1.0 / (SEQ_DEV * NZ * NH))
    for half in range(2):
        o_copy(half).wait_send()


def on_device(acts, grads, basis_in, basis_out, seq_ids):
    dma = pltpu.SemaphoreType.DMA
    ring, half, skip = dma((2, 2, 8)), dma((2, 1, 8)), dma((2, 4, 2))
    return pl.pallas_call(
        kernel,
        out_shape=jax.ShapeDtypeStruct((COLS, TOK), F32),
        in_specs=[pl.BlockSpec(memory_space=pl.ANY)] * 4 + [pl.BlockSpec(memory_space=pltpu.VMEM)],
        out_specs=pl.BlockSpec(memory_space=pltpu.VMEM),
        scratch_shapes=[
            pltpu.VMEM((NH * TOK, HALF), BF16),
            pltpu.VMEM((NH * TOK, HALF), BF16),
            pltpu.VMEM((NZ, ROWS, COLS), BF16),
            pltpu.VMEM((2, NZ, ROWS, TOK), BF16),
            pltpu.VMEM((ROWS, COLS), F32),
            pltpu.VMEM((ROWS, COLS), F32),
            pltpu.VMEM((NH * TOK, COLS), F32),
            pltpu.VMEM((2, NH * TOK, TOK), F32),
            pltpu.VMEM((TOK, COLS), BF16),
            pltpu.VMEM((TOK, COLS), BF16),
            pltpu.VMEM((2, TOK, TOK), BF16),
            pltpu.VMEM((2, TOK, TOK), BF16),
            pltpu.VMEM((2, TOK, TOK), BF16),
            pltpu.VMEM((NZ, TOK + TAG, TOK), BF16),
            pltpu.VMEM((NZ, TOK, TOK), BF16),
            pltpu.VMEM((NZ, NH, TOK, TOK), BF16),
            pltpu.VMEM((2, NH, TOK, TOK), F32),
            pltpu.VMEM((2, TOK, TOK), F32),
            dma((4,)),
            ring, ring, half, half, half, half, skip, skip, skip, skip,
            dma((2,)), dma((2,)), dma((2,)), dma((2,)), dma((3,)), dma((3,)),
            dma((2,)), dma((2,)), dma((7,)), dma((7,)), dma((8,)), dma((8,)), dma((2,)), dma((2,)),
        ],
        compiler_params=pltpu.CompilerParams(
            collective_id=0, has_side_effects=True, vmem_limit_bytes=62 * 1024 * 1024),
        cost_estimate=pl.CostEstimate(flops=3_300_000_000, bytes_accessed=8_000_000, transcendentals=0),
    )(acts, grads, basis_in, basis_out, seq_ids.reshape(1, TOK))


def solution(mesh):
    return jax.shard_map(
        on_device,
        mesh=mesh,
        in_specs=(
            P("dp", None),
            P("dp", None),
            P("dp", ("blk", "pair")),
            P("dp", ("blk", "pair")),
            P("dp"),
        ),
        out_specs=P(("blk", "pair"), "dp"),
        check_vma=False,
    )
```

time: 121 us -> 111 us (0.917)
  the two profiles are of different devices: /device:TPU:8 before, /device:TPU:6 now
where the time goes in v3:
time: 111 us
  Pallas kernels  109 us (98%)
  local copies, waits for them, and re-layouts  1.57 us (1%)
    pallas_call x1, Pallas kernels, on_device(): pl.pallas_call(kernel, out_shape=jax.ShapeDtypeStruct((COLS, TOK), F32),...  109 us

profile of v3, /device:TPU:6, one launch (start us, length us, event | category | flops | bytes accessed | tf_op | source)
XLA Modules:
  0.0 110.5 jit_solution(535464286326577640)
XLA Ops:
  0.0 109.0 %shard_map.55 = f32[256,128]{1,0:T(8,128)} custom-call(bf16[128,8192]{1,0:T(8,128)(2,1)} %acts.1, bf16[128,8192]{1,0:T(8,128)(2,1)} %grads.1, f32[256,256]{1,0:T(8,128)} %basis_in.1, f32[256,256]{1,0:T(8,128)} %basis_out.1, s32[1,128]{1,0:T(1,128)} %bitcast.1), custom_call_target="tpu_custom_call" | custom-call | flops 3300000000 | bytes 8000000 | tf_op jit(solution)/shard_map/pallas_call | solution.py:366
  109.0 1.6 %copy.7 = f32[256,128]{1,0:T(8,128)} copy(f32[256,128]{1,0:T(8,128)} %shard_map.55) | data formatting | bytes 262144

commit v4 on v3

--- a/solution.py
+++ b/solution.py
@@ -12,8 +12,8 @@
 COLS = 256
 ROWS = 256
 HALF = NZ * ROWS
-LAG_A = 2
-LAG_B = 5
+LAG_IN = 2
+LAG_B = 7
 TAG = 16
 MESH = pl.DeviceIdType.MESH
 F32 = jnp.float32
@@ -256,88 +256,90 @@
 
     for m in range(LAG_B + 9):
         if m <= 8:
-            ring_in.step(m)
-        if LAG_A <= m <= LAG_A + 8:
-            ring_a.step(m - LAG_A)
+            ring_a.step(m)
+        if LAG_IN <= m <= LAG_IN + 8:
+            ring_in.step(m - LAG_IN)
         if m >= LAG_B:
             ring_b.step(m - LAG_B)
         if m == 0:
+            y_copy(1).start()
             y_copy(0).start()
-            y_copy(1).start()
+        if m == 5:
+            y_copy(1).wait_recv()
+            k_copy(1, row0).start()
         if m == 6:
+            loads[3].wait()
+            k_copy(1, other0).wait_recv()
+            add_a(z)
+            around(1, 3, add_a)
+        if m == 7:
             y_copy(0).wait_recv()
             k_copy(0, row0).start()
-        if m == 7:
+            around(4, 6, add_a)
+        if m == 8:
+            around(7, 7, add_a)
+            add_a(opposite)
+            send_partial(0)
             loads[2].wait()
             k_copy(0, other0).wait_recv()
             add_in(z)
-            around(1, 4, add_in)
-            y_copy(1).wait_recv()
-            k_copy(1, row0).start()
-        if m == 8:
-            around(5, 7, add_in)
+            around(1, 2, add_in)
+        if m == 9:
+            gath[z, 0:TOK] = turned(0)
+            ring_ga.round(0)
+            around(3, 6, add_in)
+        if m == 10:
+            around(7, 7, add_in)
             add_in(opposite)
             psend[...] = acc[TOK:].astype(BF16)
             h_copy(0).start()
-        if m == 9:
-            loads[3].wait()
-            k_copy(1, other0).wait_recv()
-            add_a(z)
-            around(1, 6, add_a)
-        if m == 10:
+            ring_ga.round(1)
+        if m == 11:
             h_copy(0).wait_recv()
             rotated = (acc[:TOK] + precv[...].astype(F32)).astype(BF16)
             rots[0] = rotated[:, :TOK]
             rots[1] = rotated[:, TOK:]
             for q in range(2):
                 p_copy(q).start()
-            around(7, 7, add_a)
-            add_a(opposite)
-            send_partial(0)
-        if m == 11:
+            ring_ga.round(2)
+            add_b(z)
+            around(1, 3, add_b)
+        if m == 12:
+            ring_ga.round(3)
             for j in range(2):
                 p_arrive(j)
             for n in range(len(peers)):
                 q_copy(n, zc).start()
             t_copy(7, zc).start()
-            add_b(z)
-            around(1, 5, add_b)
-        if m == 12:
-            gath[z, 0:TOK] = turned(0)
-            ring_ga.round(0)
+            around(4, 5, add_b)
+        if m == 13:
+            ring_ga.round(4)
+            around(6, 6, add_b)
+        if m == 14:
             for n, (dx, dy) in enumerate(peers):
                 block = collected(dx, dy, core)
                 q_copy(n, block).wait_recv()
                 t_copy(n, block).start()
-            around(6, 7, add_b)
-        if m == 13:
+            around(7, 7, add_b)
+        if m == 15:
             add_b(opposite)
             send_partial(1)
 
-    ring_ga.round(1)
     for n, (dx, dy) in enumerate(peers):
         t_copy(n, collected(dx, dy, 1 - core)).wait_recv()
     t_copy(7, collected(0, 0, 1 - core)).wait_recv()
     squares(0, 0)
     squares(0, 1)
+    squares(0, 2)
     gath2[z] = turned(1)
     ring_gb.round(0)
-    ring_ga.round(2)
-    squares(1, 0)
-    squares(0, 2)
-    ring_gb.round(1)
-    ring_ga.round(3)
-    squares(1, 1)
     squares(0, 3)
-    ring_gb.round(2)
-    ring_ga.round(4)
     squares(0, 4)
     o_copy(0).start()
-    squares(1, 2)
-    ring_gb.round(3)
-    squares(1, 3)
-    ring_gb.round(4)
-    squares(1, 4)
+    squares(1, 0)
+    for r in range(1, 5):
+        ring_gb.round(r)
+        squares(1, r)
     o_copy(1).start()
 
     for ring in (ring_in, ring_a, ring_b, ring_ga, ring_gb):

time: 111 us -> 118 us (1.063); the launches traced: 111 us -> 116 us
  Pallas kernels: 109 us -> 114 us
    pallas_call x1, Pallas kernels: 109 us -> 114 us  [on_device(): pl.pallas_call(kernel, out_shape=jax.ShapeDtypeStruct((COLS, TOK), F32),...]
where the time goes in v4:
time: 118 us; the launch traced here: 116 us
  Pallas kernels  114 us (97%)
  local copies, waits for them, and re-layouts  1.57 us (1%)
    pallas_call x1, Pallas kernels, on_device(): pl.pallas_call(kernel, out_shape=jax.ShapeDtypeStruct((COLS, TOK), F32),...  114 us

profile of v4, /device:TPU:6, one launch (start us, length us, event | category | flops | bytes accessed | tf_op | source)
XLA Modules:
  0.0 116.0 jit_solution(13410168714834684196)
XLA Ops:
  0.0 114.4 %shard_map.55 = f32[256,128]{1,0:T(8,128)} custom-call(bf16[128,8192]{1,0:T(8,128)(2,1)} %acts.1, bf16[128,8192]{1,0:T(8,128)(2,1)} %grads.1, f32[256,256]{1,0:T(8,128)} %basis_in.1, f32[256,256]{1,0:T(8,128)} %basis_out.1, s32[1,128]{1,0:T(1,128)} %bitcast.1), custom_call_target="tpu_custom_call" | custom-call | flops 3300000000 | bytes 8000000 | tf_op jit(solution)/shard_map/pallas_call | solution.py:368
  114.4 1.6 %copy.7 = f32[256,128]{1,0:T(8,128)} copy(f32[256,128]{1,0:T(8,128)} %shard_map.55) | data formatting | bytes 262144

commit v5 on v3

--- a/solution.py
+++ b/solution.py
@@ -12,8 +12,7 @@
 COLS = 256
 ROWS = 256
 HALF = NZ * ROWS
-LAG_A = 2
-LAG_B = 5
+LAG_B = 4
 TAG = 16
 MESH = pl.DeviceIdType.MESH
 F32 = jnp.float32
@@ -148,8 +147,6 @@
     tags = jnp.bitwise_and(seq[...], SEQ_DEV - 1).astype(F32)
     gath[z, TOK:TOK + TAG] = jnp.broadcast_to(tags, (TAG, TOK)).astype(BF16)
     osum[...] = jnp.zeros_like(osum)
-    acc[...] = jnp.zeros_like(acc)
-    accs[...] = jnp.zeros_like(accs)
 
     pl.semaphore_wait(barrier, len(greet))
 
@@ -207,27 +204,6 @@
         return pltpu.make_async_remote_copy(
             src_ref=piece, dst_ref=piece, send_sem=t_s.at[n], recv_sem=t_r.at[n],
             device_id=sibling, device_id_type=MESH)
-
-    def add_in(slot):
-        columns = pl.ds(pl.multiple_of(slot * ROWS, ROWS), ROWS)
-        acc[...] += jnp.dot(a_in[:, columns], b_in[slot], preferred_element_type=F32)
-
-    def add_out(half, slot):
-        columns = pl.ds(pl.multiple_of(slot * ROWS, ROWS), ROWS)
-        accs[half] += jnp.dot(a_out[:, columns], b_out[half, slot], preferred_element_type=F32)
-
-    def around(near, far, add):
-        @pl.loop(2 * near, 2 * far + 2)
-        def _(n):
-            add(lax.rem(z + NZ + (2 * lax.rem(n, 2) - 1) * (n // 2), NZ))
-
-    def add_a(slot):
-        add_out(0, slot)
-
-    def add_b(slot):
-        add_out(1, slot)
-
-    opposite = lax.rem(z + NZ // 2, NZ)
 
     def square(half, slot):
         left = gath[slot, 0:TOK] if half == 0 else gath2[slot]
@@ -247,6 +223,7 @@
             square(half, slot)
 
     def send_partial(half):
+        accs[half] = jnp.dot(a_out[...], b_out[half].reshape(HALF, TOK), preferred_element_type=F32)
         psends[half] = accs[half, TOK:].astype(BF16)
         h_copy(1 + half).start()
 
@@ -257,8 +234,7 @@
     for m in range(LAG_B + 9):
         if m <= 8:
             ring_in.step(m)
-        if LAG_A <= m <= LAG_A + 8:
-            ring_a.step(m - LAG_A)
+            ring_a.step(m)
         if m >= LAG_B:
             ring_b.step(m - LAG_B)
         if m == 0:
@@ -268,53 +244,42 @@
             y_copy(0).wait_recv()
             k_copy(0, row0).start()
         if m == 7:
-            loads[2].wait()
-            k_copy(0, other0).wait_recv()
-            add_in(z)
-            around(1, 4, add_in)
             y_copy(1).wait_recv()
             k_copy(1, row0).start()
         if m == 8:
-            around(5, 7, add_in)
-            add_in(opposite)
+            loads[3].wait()
+            k_copy(1, other0).wait_recv()
+            send_partial(0)
+            loads[2].wait()
+            k_copy(0, other0).wait_recv()
+            acc[...] = jnp.dot(a_in[...], b_in[...].reshape(HALF, COLS), preferred_element_type=F32)
             psend[...] = acc[TOK:].astype(BF16)
             h_copy(0).start()
-        if m == 9:
-            loads[3].wait()
-            k_copy(1, other0).wait_recv()
-            add_a(z)
-            around(1, 6, add_a)
         if m == 10:
+            gath[z, 0:TOK] = turned(0)
+            ring_ga.round(0)
             h_copy(0).wait_recv()
             rotated = (acc[:TOK] + precv[...].astype(F32)).astype(BF16)
             rots[0] = rotated[:, :TOK]
             rots[1] = rotated[:, TOK:]
             for q in range(2):
                 p_copy(q).start()
-            around(7, 7, add_a)
-            add_a(opposite)
-            send_partial(0)
         if m == 11:
+            ring_ga.round(1)
             for j in range(2):
                 p_arrive(j)
             for n in range(len(peers)):
                 q_copy(n, zc).start()
             t_copy(7, zc).start()
-            add_b(z)
-            around(1, 5, add_b)
         if m == 12:
-            gath[z, 0:TOK] = turned(0)
-            ring_ga.round(0)
-            for n, (dx, dy) in enumerate(peers):
-                block = collected(dx, dy, core)
-                q_copy(n, block).wait_recv()
-                t_copy(n, block).start()
-            around(6, 7, add_b)
-        if m == 13:
-            add_b(opposite)
-            send_partial(1)
-
-    ring_ga.round(1)
+            ring_ga.round(2)
+    send_partial(1)
+
+    for n, (dx, dy) in enumerate(peers):
+        block = collected(dx, dy, core)
+        q_copy(n, block).wait_recv()
+        t_copy(n, block).start()
+    ring_ga.round(3)
     for n, (dx, dy) in enumerate(peers):
         t_copy(n, collected(dx, dy, 1 - core)).wait_recv()
     t_copy(7, collected(0, 0, 1 - core)).wait_recv()
@@ -322,22 +287,17 @@
     squares(0, 1)
     gath2[z] = turned(1)
     ring_gb.round(0)
-    ring_ga.round(2)
-    squares(1, 0)
+    ring_ga.round(4)
     squares(0, 2)
+    squares(0, 3)
     ring_gb.round(1)
-    ring_ga.round(3)
-    squares(1, 1)
-    squares(0, 3)
-    ring_gb.round(2)
-    ring_ga.round(4)
     squares(0, 4)
     o_copy(0).start()
-    squares(1, 2)
-    ring_gb.round(3)
-    squares(1, 3)
-    ring_gb.round(4)
-    squares(1, 4)
+    squares(1, 0)
+    squares(1, 1)
+    for r in range(2, 5):
+        ring_gb.round(r)
+        squares(1, r)
     o_copy(1).start()
 
     for ring in (ring_in, ring_a, ring_b, ring_ga, ring_gb):

time: 111 us -> 114 us (1.027); the launches traced: 111 us -> 112 us
    pallas_call x1, Pallas kernels: 109 us -> 110 us  [on_device(): pl.pallas_call(kernel, out_shape=jax.ShapeDtypeStruct((COLS, TOK), F32),...]
where the time goes in v5:
time: 114 us; the launch traced here: 112 us
  Pallas kernels  110 us (96%)
  local copies, waits for them, and re-layouts  1.57 us (1%)
    pallas_call x1, Pallas kernels, on_device(): pl.pallas_call(kernel, out_shape=jax.ShapeDtypeStruct((COLS, TOK), F32),...  110 us

profile of v5, /device:TPU:6, one launch (start us, length us, event | category | flops | bytes accessed | tf_op | source)
XLA Modules:
  0.0 111.9 jit_solution(12731683943309796979)
XLA Ops:
  0.0 110.4 %shard_map.55 = f32[256,128]{1,0:T(8,128)} custom-call(bf16[128,8192]{1,0:T(8,128)(2,1)} %acts.1, bf16[128,8192]{1,0:T(8,128)(2,1)} %grads.1, f32[256,256]{1,0:T(8,128)} %basis_in.1, f32[256,256]{1,0:T(8,128)} %basis_out.1, s32[1,128]{1,0:T(1,128)} %bitcast.1), custom_call_target="tpu_custom_call" | custom-call | flops 3300000000 | bytes 8000000 | tf_op jit(solution)/shard_map/pallas_call | solution.py:326
  110.4 1.6 %copy.7 = f32[256,128]{1,0:T(8,128)} copy(f32[256,128]{1,0:T(8,128)} %shard_map.55) | data formatting | bytes 262144

commit v6 on v5

--- a/solution.py
+++ b/solution.py
@@ -93,7 +93,7 @@
            a_in, a_out, b_in, b_out, f_in, f_out, acc, accs, psend, precv, psends, precvs, rots, gath, gath2, right,
            osum, orecv,
            load, in_s, in_r, out_s, out_r, out2_s, out2_r, g_s, g_r, g2_s, g2_r,
-           y_s, y_r, k_s, k_r, h_s, h_r, p_s, p_r, q_s, q_r, t_s, t_r, o_s, o_r):
+           y_s, y_r, x_s, x_r, k_s, k_r, h_s, h_r, p_s, p_r, q_s, q_r, t_s, t_r, o_s, o_r):
     blk, pair, dp = lax.axis_index("blk"), lax.axis_index("pair"), lax.axis_index("dp")
     x, core = blk // 2, lax.rem(blk, 2)
     h, z = dp // NZ, lax.rem(dp, NZ)
@@ -158,10 +158,19 @@
     ring_ga = Skip(lambda slot: gath.at[slot], (8, 7), g_s, g_r, h, z)
     ring_gb = Skip(lambda slot: gath2.at[slot], (7, 8), g2_s, g2_r, h, z)
 
+    def yrow(dx):
+        return pl.multiple_of(core * 64 + lax.rem(x - dx + 4, 4) * 16, 16)
+
+    def x_copy(i, dx, first):
+        piece = (a_in, a_out)[i].at[pl.ds(TOK + first, 16)]
+        return pltpu.make_async_remote_copy(
+            src_ref=piece, dst_ref=piece, send_sem=x_s.at[i, dx - 1], recv_sem=x_r.at[i, dx - 1],
+            device_id=peer(dx, 0), device_id_type=MESH)
+
     def y_copy(i):
         source, held = ((acts, a_in), (grads, a_out))[i]
         return pltpu.make_async_remote_copy(
-            src_ref=source.at[pl.ds(row0, 64), theirs], dst_ref=held.at[pl.ds(TOK + row0, 64)],
+            src_ref=source.at[pl.ds(yrow(0), 16), theirs], dst_ref=held.at[pl.ds(TOK + yrow(0), 16)],
             send_sem=y_s.at[i], recv_sem=y_r.at[i], device_id=across, device_id_type=MESH)
 
     def k_copy(i, first):
@@ -240,12 +249,16 @@
         if m == 0:
             y_copy(0).start()
             y_copy(1).start()
+        if m == 3:
+            for i in range(2):
+                y_copy(i).wait_recv()
+                for dx in range(1, 4):
+                    x_copy(i, dx, yrow(0)).start()
         if m == 6:
-            y_copy(0).wait_recv()
-            k_copy(0, row0).start()
-        if m == 7:
-            y_copy(1).wait_recv()
-            k_copy(1, row0).start()
+            for i in range(2):
+                for dx in range(1, 4):
+                    x_copy(i, dx, yrow(dx)).wait_recv()
+                k_copy(i, row0).start()
         if m == 8:
             loads[3].wait()
             k_copy(1, other0).wait_recv()
@@ -304,6 +317,8 @@
         ring.finish()
     for i in range(2):
         y_copy(i).wait_send()
+        for dx in range(1, 4):
+            x_copy(i, dx, yrow(0)).wait_send()
         k_copy(i, row0).wait_send()
         p_copy(i).wait_send()
     for i in range(3):
@@ -349,7 +364,7 @@
             pltpu.VMEM((2, TOK, TOK), F32),
             dma((4,)),
             ring, ring, half, half, half, half, skip, skip, skip, skip,
-            dma((2,)), dma((2,)), dma((2,)), dma((2,)), dma((3,)), dma((3,)),
+            dma((2,)), dma((2,)), dma((2, 3)), dma((2, 3)), dma((2,)), dma((2,)), dma((3,)), dma((3,)),
             dma((2,)), dma((2,)), dma((7,)), dma((7,)), dma((8,)), dma((8,)), dma((2,)), dma((2,)),
         ],
         compiler_params=pltpu.CompilerParams(

time: 114 us -> 114 us (level)
  no operation moved by 1% of the time
where the time goes in v6:
time: 114 us; the launch traced here: 112 us
  Pallas kernels  111 us (97%)
  local copies, waits for them, and re-layouts  1.57 us (1%)
    pallas_call x1, Pallas kernels, on_device(): pl.pallas_call(kernel, out_shape=jax.ShapeDtypeStruct((COLS, TOK), F32),...  111 us

profile of v6, /device:TPU:6, one launch (start us, length us, event | category | flops | bytes accessed | tf_op | source)
XLA Modules:
  0.0 112.2 jit_solution(6428055868190054955)
XLA Ops:
  0.0 110.6 %shard_map.55 = f32[256,128]{1,0:T(8,128)} custom-call(bf16[128,8192]{1,0:T(8,128)(2,1)} %acts.1, bf16[128,8192]{1,0:T(8,128)(2,1)} %grads.1, f32[256,256]{1,0:T(8,128)} %basis_in.1, f32[256,256]{1,0:T(8,128)} %basis_out.1, s32[1,128]{1,0:T(1,128)} %bitcast.1), custom_call_target="tpu_custom_call" | custom-call | flops 3300000000 | bytes 8000000 | tf_op jit(solution)/shard_map/pallas_call | solution.py:341
  110.6 1.6 %copy.7 = f32[256,128]{1,0:T(8,128)} copy(f32[256,128]{1,0:T(8,128)} %shard_map.55) | data formatting | bytes 262144

commit v7 on v5

--- a/solution.py
+++ b/solution.py
@@ -147,13 +147,13 @@
     tags = jnp.bitwise_and(seq[...], SEQ_DEV - 1).astype(F32)
     gath[z, TOK:TOK + TAG] = jnp.broadcast_to(tags, (TAG, TOK)).astype(BF16)
     osum[...] = jnp.zeros_like(osum)
+    acc[...] = jnp.zeros_like(acc)
+    accs[...] = jnp.zeros_like(accs)
 
     pl.semaphore_wait(barrier, len(greet))
 
-    part_rows = ROWS // 2
-    ring_in = Ring(lambda part, slot: b_in.at[slot, pl.ds(part * part_rows, part_rows)],
-                   ((8, 7), (7, 8)), in_s, in_r, h, z)
-    ring_a = Ring(lambda part, slot: b_out.at[0, slot], ((8, 7),), out_s, out_r, h, z)
+    ring_in = Ring(lambda part, slot: b_in.at[slot], ((8, 7),), in_s, in_r, h, z)
+    ring_a = Ring(lambda part, slot: b_out.at[0, slot], ((7, 8),), out_s, out_r, h, z)
     ring_b = Ring(lambda part, slot: b_out.at[1, slot], ((7, 8),), out2_s, out2_r, h, z)
     ring_ga = Skip(lambda slot: gath.at[slot], (8, 7), g_s, g_r, h, z)
     ring_gb = Skip(lambda slot: gath2.at[slot], (7, 8), g2_s, g2_r, h, z)
@@ -204,6 +204,27 @@
         return pltpu.make_async_remote_copy(
             src_ref=piece, dst_ref=piece, send_sem=t_s.at[n], recv_sem=t_r.at[n],
             device_id=sibling, device_id_type=MESH)
+
+    def add_in(slot):
+        columns = pl.ds(pl.multiple_of(slot * ROWS, ROWS), ROWS)
+        acc[...] += jnp.dot(a_in[:, columns], b_in[slot], preferred_element_type=F32)
+
+    def add_out(half, slot):
+        columns = pl.ds(pl.multiple_of(slot * ROWS, ROWS), ROWS)
+        accs[half] += jnp.dot(a_out[:, columns], b_out[half, slot], preferred_element_type=F32)
+
+    def around(near, far, add):
+        @pl.loop(2 * near, 2 * far + 2)
+        def _(n):
+            add(lax.rem(z + NZ + (2 * lax.rem(n, 2) - 1) * (n // 2), NZ))
+
+    def add_a(slot):
+        add_out(0, slot)
+
+    def add_b(slot):
+        add_out(1, slot)
+
+    opposite = lax.rem(z + NZ // 2, NZ)
 
     def square(half, slot):
         left = gath[slot, 0:TOK] if half == 0 else gath2[slot]
@@ -223,7 +244,6 @@
             square(half, slot)
 
     def send_partial(half):
-        accs[half] = jnp.dot(a_out[...], b_out[half].reshape(HALF, TOK), preferred_element_type=F32)
         psends[half] = accs[half, TOK:].astype(BF16)
         h_copy(1 + half).start()
 
@@ -241,20 +261,30 @@
             y_copy(0).start()
             y_copy(1).start()
         if m == 6:
-            y_copy(0).wait_recv()
-            k_copy(0, row0).start()
+            for i in (1, 0):
+                y_copy(i).wait_recv()
+                k_copy(i, row0).start()
         if m == 7:
-            y_copy(1).wait_recv()
-            k_copy(1, row0).start()
-        if m == 8:
             loads[3].wait()
             k_copy(1, other0).wait_recv()
-            send_partial(0)
+            add_a(z)
+            around(1, 4, add_a)
             loads[2].wait()
             k_copy(0, other0).wait_recv()
-            acc[...] = jnp.dot(a_in[...], b_in[...].reshape(HALF, COLS), preferred_element_type=F32)
+            add_in(z)
+            around(1, 4, add_in)
+        if m == 8:
+            around(5, 7, add_a)
+            add_a(opposite)
+            send_partial(0)
+            around(5, 7, add_in)
+            add_in(opposite)
             psend[...] = acc[TOK:].astype(BF16)
             h_copy(0).start()
+        if m == 9:
+            add_b(z)
+            around(1, 4, add_b)
+            ring_in.finish()
         if m == 10:
             gath[z, 0:TOK] = turned(0)
             ring_ga.round(0)
@@ -271,43 +301,51 @@
             for n in range(len(peers)):
                 q_copy(n, zc).start()
             t_copy(7, zc).start()
+            around(5, 6, add_b)
         if m == 12:
+            around(7, 7, add_b)
+            add_b(opposite)
+            send_partial(1)
             ring_ga.round(2)
-    send_partial(1)
 
     for n, (dx, dy) in enumerate(peers):
         block = collected(dx, dy, core)
         q_copy(n, block).wait_recv()
         t_copy(n, block).start()
     ring_ga.round(3)
+    gath2[z] = turned(1)
+    ring_gb.round(0)
     for n, (dx, dy) in enumerate(peers):
         t_copy(n, collected(dx, dy, 1 - core)).wait_recv()
     t_copy(7, collected(0, 0, 1 - core)).wait_recv()
     squares(0, 0)
     squares(0, 1)
-    gath2[z] = turned(1)
-    ring_gb.round(0)
     ring_ga.round(4)
     squares(0, 2)
+    ring_gb.round(1)
     squares(0, 3)
-    ring_gb.round(1)
     squares(0, 4)
     o_copy(0).start()
     squares(1, 0)
+    ring_gb.round(2)
     squares(1, 1)
-    for r in range(2, 5):
-        ring_gb.round(r)
-        squares(1, r)
-    o_copy(1).start()
-
-    for ring in (ring_in, ring_a, ring_b, ring_ga, ring_gb):
-        ring.finish()
+    ring_a.finish()
+    ring_gb.round(3)
+    squares(1, 2)
     for i in range(2):
         y_copy(i).wait_send()
         k_copy(i, row0).wait_send()
         p_copy(i).wait_send()
     for i in range(3):
         h_copy(i).wait_send()
+    ring_gb.round(4)
+    squares(1, 3)
+    squares(1, 4)
+    o_copy(1).start()
+
+    ring_b.finish()
+    ring_ga.finish()
+    ring_gb.finish()
     for n, (dx, dy) in enumerate(peers):
         q_copy(n, zc).wait_send()
         t_copy(n, collected(dx, dy, core)).wait_send()
@@ -322,7 +360,7 @@
 
 def on_device(acts, grads, basis_in, basis_out, seq_ids):
     dma = pltpu.SemaphoreType.DMA
-    ring, half, skip = dma((2, 2, 8)), dma((2, 1, 8)), dma((2, 4, 2))
+    half, skip = dma((2, 1, 8)), dma((2, 4, 2))
     return pl.pallas_call(
         kernel,
         out_shape=jax.ShapeDtypeStruct((COLS, TOK), F32),
@@ -348,7 +386,7 @@
             pltpu.VMEM((2, NH, TOK, TOK), F32),
             pltpu.VMEM((2, TOK, TOK), F32),
             dma((4,)),
-            ring, ring, half, half, half, half, skip, skip, skip, skip,
+            half, half, half, half, half, half, skip, skip, skip, skip,
             dma((2,)), dma((2,)), dma((2,)), dma((2,)), dma((3,)), dma((3,)),
             dma((2,)), dma((2,)), dma((7,)), dma((7,)), dma((8,)), dma((8,)), dma((2,)), dma((2,)),
         ],

time: 114 us -> 114 us (level)
  no operation moved by 1% of the time
where the time goes in v7:
time: 114 us; the launch traced here: 113 us
  Pallas kernels  111 us (97%)
  local copies, waits for them, and re-layouts  1.57 us (1%)
    pallas_call x1, Pallas kernels, on_device(): pl.pallas_call(kernel, out_shape=jax.ShapeDtypeStruct((COLS, TOK), F32),...  111 us

profile of v7, /device:TPU:6, one launch (start us, length us, event | category | flops | bytes accessed | tf_op | source)
XLA Modules:
  0.0 112.6 jit_solution(17140742511450942371)
XLA Ops:
  0.0 111.0 %shard_map.55 = f32[256,128]{1,0:T(8,128)} custom-call(bf16[128,8192]{1,0:T(8,128)(2,1)} %acts.1, bf16[128,8192]{1,0:T(8,128)(2,1)} %grads.1, f32[256,256]{1,0:T(8,128)} %basis_in.1, f32[256,256]{1,0:T(8,128)} %basis_out.1, s32[1,128]{1,0:T(1,128)} %bitcast.1), custom_call_target="tpu_custom_call" | custom-call | flops 3300000000 | bytes 8000000 | tf_op jit(solution)/shard_map/pallas_call | solution.py:364
  111.0 1.6 %copy.7 = f32[256,128]{1,0:T(8,128)} copy(f32[256,128]{1,0:T(8,128)} %shard_map.55) | data formatting | bytes 262144

commit v8 on v3

--- a/solution.py
+++ b/solution.py
@@ -99,8 +99,8 @@
     x, core = blk // 2, lax.rem(blk, 2)
     h, z = dp // NZ, lax.rem(dp, NZ)
     c = blk * 2 + pair
-    zc = lax.rem(lax.rem(c, 8) + 7, 8) * 2 + c // 8
-    cz = lax.rem(z // 2 + 1, 8) + 8 * lax.rem(z, 2)
+    zc = lax.rem(c + z // 2 + NZ - 2, NZ)
+    cz = lax.rem(z - lax.rem(c, 8) + 2 + NZ, NZ)
     row0 = pl.multiple_of(core * 64, 64)
     other0 = pl.multiple_of((1 - core) * 64, 64)
 
@@ -114,7 +114,7 @@
 
     def collected(dx, dy, k):
         of = (lax.rem(x - dx + 4, 4) * 2 + k) * 2 + lax.rem(pair + dy, 2)
-        return lax.rem(lax.rem(of, 8) + 7, 8) * 2 + of // 8
+        return lax.rem(of + z // 2 + NZ - 2, NZ)
 
     mine = pl.ds(pl.multiple_of(h * HALF, HALF), HALF)
     theirs = pl.ds(pl.multiple_of((1 - h) * HALF, HALF), HALF)
@@ -315,39 +315,40 @@
             send_partial(1)
 
     ring_ga.round(1)
+    ring_in.finish()
+    gath2[z] = turned(1)
+    ring_gb.round(0)
+    ring_ga.round(2)
     for n, (dx, dy) in enumerate(peers):
         t_copy(n, collected(dx, dy, 1 - core)).wait_recv()
     t_copy(7, collected(0, 0, 1 - core)).wait_recv()
     squares(0, 0)
     squares(0, 1)
-    gath2[z] = turned(1)
-    ring_gb.round(0)
-    ring_ga.round(2)
-    squares(1, 0)
-    squares(0, 2)
     ring_gb.round(1)
     ring_ga.round(3)
-    squares(1, 1)
+    squares(0, 2)
     squares(0, 3)
     ring_gb.round(2)
     ring_ga.round(4)
     squares(0, 4)
     o_copy(0).start()
+    squares(1, 0)
+    squares(1, 1)
+    ring_gb.round(3)
     squares(1, 2)
-    ring_gb.round(3)
-    squares(1, 3)
-    ring_gb.round(4)
-    squares(1, 4)
-    o_copy(1).start()
-
-    for ring in (ring_in, ring_a, ring_b, ring_ga, ring_gb):
-        ring.finish()
     for i in range(2):
         y_copy(i).wait_send()
         k_copy(i, row0).wait_send()
         p_copy(i).wait_send()
     for i in range(3):
         h_copy(i).wait_send()
+    ring_gb.round(4)
+    squares(1, 3)
+    squares(1, 4)
+    o_copy(1).start()
+
+    for ring in (ring_a, ring_b, ring_ga, ring_gb):
+        ring.finish()
     for n, (dx, dy) in enumerate(peers):
         q_copy(n, zc).wait_send()
         t_copy(n, collected(dx, dy, core)).wait_send()

time: 111 us -> 113 us (1.018)
    pallas_call x1, Pallas kernels: 109 us -> 110 us  [on_device(): pl.pallas_call(kernel, out_shape=jax.ShapeDtypeStruct((COLS, TOK), F32),...]
where the time goes in v8:
time: 113 us; the launch traced here: 112 us
  Pallas kernels  110 us (97%)
  local copies, waits for them, and re-layouts  1.57 us (1%)
    pallas_call x1, Pallas kernels, on_device(): pl.pallas_call(kernel, out_shape=jax.ShapeDtypeStruct((COLS, TOK), F32),...  110 us

profile of v8, /device:TPU:6, one launch (start us, length us, event | category | flops | bytes accessed | tf_op | source)
XLA Modules:
  0.0 112.0 jit_solution(14828621128908220531)
XLA Ops:
  0.0 110.4 %shard_map.55 = f32[256,128]{1,0:T(8,128)} custom-call(bf16[128,8192]{1,0:T(8,128)(2,1)} %acts.1, bf16[128,8192]{1,0:T(8,128)(2,1)} %grads.1, f32[256,256]{1,0:T(8,128)} %basis_in.1, f32[256,256]{1,0:T(8,128)} %basis_out.1, s32[1,128]{1,0:T(1,128)} %bitcast.1), custom_call_target="tpu_custom_call" | custom-call | flops 3300000000 | bytes 8000000 | tf_op jit(solution)/shard_map/pallas_call | solution.py:367
  110.4 1.6 %copy.7 = f32[256,128]{1,0:T(8,128)} copy(f32[256,128]{1,0:T(8,128)} %shard_map.55) | data formatting | bytes 262144

commit v9 on v8

--- a/solution.py
+++ b/solution.py
@@ -284,31 +284,27 @@
             k_copy(1, other0).wait_recv()
             add_a(z)
             around(1, 6, add_a)
-        if m == 10:
             h_copy(0).wait_recv()
             rotated = (acc[:TOK] + precv[...].astype(F32)).astype(BF16)
             rots[0] = rotated[:, :TOK]
             rots[1] = rotated[:, TOK:]
             for q in range(2):
                 p_copy(q).start()
+        if m == 10:
             around(7, 7, add_a)
             add_a(opposite)
             send_partial(0)
         if m == 11:
+            add_b(z)
+            around(1, 5, add_b)
             for j in range(2):
                 p_arrive(j)
             for n in range(len(peers)):
                 q_copy(n, zc).start()
             t_copy(7, zc).start()
-            add_b(z)
-            around(1, 5, add_b)
         if m == 12:
             gath[z, 0:TOK] = turned(0)
             ring_ga.round(0)
-            for n, (dx, dy) in enumerate(peers):
-                block = collected(dx, dy, core)
-                q_copy(n, block).wait_recv()
-                t_copy(n, block).start()
             around(6, 7, add_b)
         if m == 13:
             add_b(opposite)
@@ -320,16 +316,20 @@
     ring_gb.round(0)
     ring_ga.round(2)
     for n, (dx, dy) in enumerate(peers):
+        block = collected(dx, dy, core)
+        q_copy(n, block).wait_recv()
+        t_copy(n, block).start()
+    ring_gb.round(1)
+    ring_ga.round(3)
+    for n, (dx, dy) in enumerate(peers):
         t_copy(n, collected(dx, dy, 1 - core)).wait_recv()
     t_copy(7, collected(0, 0, 1 - core)).wait_recv()
     squares(0, 0)
     squares(0, 1)
-    ring_gb.round(1)
-    ring_ga.round(3)
     squares(0, 2)
-    squares(0, 3)
     ring_gb.round(2)
     ring_ga.round(4)
+    squares(0, 3)
     squares(0, 4)
     o_copy(0).start()
     squares(1, 0)

time: 113 us -> 108 us (0.956)
  Pallas kernels: 110 us -> 106 us
    pallas_call x1, Pallas kernels: 110 us -> 106 us  [on_device(): pl.pallas_call(kernel, out_shape=jax.ShapeDtypeStruct((COLS, TOK), F32),...]
where the time goes in v9:
time: 108 us; the launch traced here: 107 us
  Pallas kernels  106 us (98%)
  local copies, waits for them, and re-layouts  1.57 us (1%)
    pallas_call x1, Pallas kernels, on_device(): pl.pallas_call(kernel, out_shape=jax.ShapeDtypeStruct((COLS, TOK), F32),...  106 us

profile of v9, /device:TPU:6, one launch (start us, length us, event | category | flops | bytes accessed | tf_op | source)
XLA Modules:
  0.0 107.1 jit_solution(5305786943841223985)
XLA Ops:
  0.0 105.5 %shard_map.55 = f32[256,128]{1,0:T(8,128)} custom-call(bf16[128,8192]{1,0:T(8,128)(2,1)} %acts.1, bf16[128,8192]{1,0:T(8,128)(2,1)} %grads.1, f32[256,256]{1,0:T(8,128)} %basis_in.1, f32[256,256]{1,0:T(8,128)} %basis_out.1, s32[1,128]{1,0:T(1,128)} %bitcast.1), custom_call_target="tpu_custom_call" | custom-call | flops 3300000000 | bytes 8000000 | tf_op jit(solution)/shard_map/pallas_call | solution.py:367
  105.5 1.6 %copy.7 = f32[256,128]{1,0:T(8,128)} copy(f32[256,128]{1,0:T(8,128)} %shard_map.55) | data formatting | bytes 262144

commit v10 on v9

--- a/solution.py
+++ b/solution.py
@@ -311,7 +311,8 @@
             send_partial(1)
 
     ring_ga.round(1)
-    ring_in.finish()
+    for ring in (ring_in, ring_a, ring_b):
+        ring.finish()
     gath2[z] = turned(1)
     ring_gb.round(0)
     ring_ga.round(2)
@@ -336,6 +337,7 @@
     squares(1, 1)
     ring_gb.round(3)
     squares(1, 2)
+    squares(1, 3)
     for i in range(2):
         y_copy(i).wait_send()
         k_copy(i, row0).wait_send()
@@ -343,11 +345,10 @@
     for i in range(3):
         h_copy(i).wait_send()
     ring_gb.round(4)
-    squares(1, 3)
     squares(1, 4)
     o_copy(1).start()
 
-    for ring in (ring_a, ring_b, ring_ga, ring_gb):
+    for ring in (ring_ga, ring_gb):
         ring.finish()
     for n, (dx, dy) in enumerate(peers):
         q_copy(n, zc).wait_send()

time: 108 us -> 108 us (level)
  no operation moved by 1% of the time
where the time goes in v10:
time: 108 us; the launch traced here: 107 us
  Pallas kernels  105 us (97%)
  local copies, waits for them, and re-layouts  1.57 us (1%)
    pallas_call x1, Pallas kernels, on_device(): pl.pallas_call(kernel, out_shape=jax.ShapeDtypeStruct((COLS, TOK), F32),...  105 us

profile of v10, /device:TPU:6, one launch (start us, length us, event | category | flops | bytes accessed | tf_op | source)
XLA Modules:
  0.0 106.8 jit_solution(853693137364398958)
XLA Ops:
  0.0 105.2 %shard_map.55 = f32[256,128]{1,0:T(8,128)} custom-call(bf16[128,8192]{1,0:T(8,128)(2,1)} %acts.1, bf16[128,8192]{1,0:T(8,128)(2,1)} %grads.1, f32[256,256]{1,0:T(8,128)} %basis_in.1, f32[256,256]{1,0:T(8,128)} %basis_out.1, s32[1,128]{1,0:T(1,128)} %bitcast.1), custom_call_target="tpu_custom_call" | custom-call | flops 3300000000 | bytes 8000000 | tf_op jit(solution)/shard_map/pallas_call | solution.py:368
  105.3 1.6 %copy.7 = f32[256,128]{1,0:T(8,128)} copy(f32[256,128]{1,0:T(8,128)} %shard_map.55) | data formatting | bytes 262144
